TPU v7x, 32 devices: a whole 2x2x4 slice. The times are simulated.
32 devices in a mesh: grp: 4 (over x, core), blk: 8 (over z, y).
Axes of the slice: x: 2, y: 2, z: 4, core: 2. Of those that a mesh axis runs over, the one named last changes fastest.
Arguments:
- query: bfloat16 [8192, 512], P(('grp', 'blk')), may hold values from -6 to 6
- key: bfloat16 [8192, 512], P(('grp', 'blk')), may hold values from -6 to 6
- value: bfloat16 [8192, 512], P(('grp', 'blk')), may hold values from -6 to 6
- out_grad: bfloat16 [8192, 512], P(('grp', 'blk')), may hold values from -6 to 6
- partner: int32 [2, 8192], P(None, ('grp', 'blk')), may hold values from 0 to 127, as said below
- tiles: int32 [64, 6], P(('grp', 'blk')), may hold values from 0 to 15, as said below
- tile_count: int32 [64], P(('grp', 'blk')), may hold values from 1 to 6, as said below
Outputs:
- attended: bfloat16 [8192, 512], P(('grp', 'blk'))
- query_grad: bfloat16 [8192, 512], P(('grp', 'blk'))
- key_grad: bfloat16 [8192, 512], P(('grp', 'blk'))
- value_grad: bfloat16 [8192, 512], P(('grp', 'blk'))
Inputs may be any that keep to these rules, and one draw needn't show every extreme that they name: `partner`: the matching of every round is symmetric: match[r, match[r, n]] = n for every node n. `tiles`: the entries of a row are distinct; the first entry of block k's row is k's own block within its cluster; block a lists block b among its first tile_count entries exactly when b lists a. `tile_count`: some block of every cluster uses all 6 slots.
All inputs are finite; a program needn't handle non-finite values.
Results may differ from a plain program's by a relative error of at most 0.014.
Values may be sent and summed in bfloat16 or wider, within the bound.
A program may use at most 64 MiB of HBM per device.

v0:
```python
import jax
import jax.numpy as jnp
from jax import lax
from jax.sharding import PartitionSpec as P

HEADS = 8
BLOCK = 128
TMAX = 6
ROUNDS = 2


NEG_BIG = -1e30


def passed_along(x, axis, by):
    size = lax.axis_size(axis)
    return lax.ppermute(x, axis, [(i, (i + by) % size) for i in range(size)])


def settle(values):
    return lax.optimization_barrier(values.astype(jnp.bfloat16)).astype(jnp.float32)


def move_rows(load, offset):
    return passed_along(load, "grp", offset)


def move_terms(load, offset):
    return passed_along(load, "grp", offset)


def fetch_partners(load, slots, offset, mover):
    half = load.shape[0] // 2
    ahead = mover(load[half:], -offset)
    behind = mover(load[:half], offset)
    return jnp.concatenate([ahead[slots[:half]], behind[slots[half:]]], 0)


def join_heads(stack):
    moved = jnp.moveaxis(stack, 0, -2)
    return moved.reshape(moved.shape[:-2] + (moved.shape[-2] * moved.shape[-1],))


def shards(query, key, value, out_grad, partner, tiles, tile_count):
    f32 = jnp.float32
    bf16 = jnp.bfloat16
    nodes, width = query.shape
    head_dim = width // HEADS
    scale = head_dim ** (-0.5)
    span = min(width, 128)
    groups = width // span
    per_group = span // head_dim
    blocks_dev = nodes // BLOCK
    team = lax.axis_size("blk")
    cluster_blocks = blocks_dev * team
    keys_tile = TMAX * BLOCK
    both = jnp.concatenate([key, value], 1)
    cluster_rows = lax.all_gather(both, "blk", axis=0, tiled=True)
    partner_rows = jnp.stack(
        [fetch_partners(both, partner[step], step + 1, move_rows) for step in range(ROUNDS)]
    )
    tiled = cluster_rows.reshape(cluster_blocks, BLOCK, 2 * width)[tiles]
    live = jnp.arange(TMAX, dtype=jnp.int32)[None, :] < tile_count[:, None]
    key_live = jnp.broadcast_to(live[:, :, None], (blocks_dev, TMAX, BLOCK)).reshape(
        blocks_dev, keys_tile
    )

    def head_group(index):
        left = index * span
        right = width + index * span
        q_part = lax.dynamic_slice_in_dim(query, left, span, 1).reshape(
            blocks_dev, BLOCK, per_group, head_dim
        )
        g_part = lax.dynamic_slice_in_dim(out_grad, left, span, 1).reshape(
            blocks_dev, BLOCK, per_group, head_dim
        )
        k_tile = lax.dynamic_slice_in_dim(tiled, left, span, 3).reshape(
            blocks_dev, keys_tile, per_group, head_dim
        )
        v_tile = lax.dynamic_slice_in_dim(tiled, right, span, 3).reshape(
            blocks_dev, keys_tile, per_group, head_dim
        )
        pair_shape = (ROUNDS, blocks_dev, BLOCK, per_group, head_dim)
        k_pair = lax.dynamic_slice_in_dim(partner_rows, left, span, 2).reshape(pair_shape)
        v_pair = lax.dynamic_slice_in_dim(partner_rows, right, span, 2).reshape(pair_shape)
        s_loc = jnp.einsum("bqhd,bkhd->bhqk", q_part, k_tile, preferred_element_type=f32) * scale
        s_loc = jnp.where(key_live[:, None, None, :], s_loc, NEG_BIG)
        s_pair = jnp.einsum("bqhd,rbqhd->bhqr", q_part, k_pair, preferred_element_type=f32) * scale
        top = jnp.maximum(jnp.max(s_loc, -1), jnp.max(s_pair, -1))
        e_loc = jnp.exp(s_loc - top[..., None])
        e_pair = jnp.exp(s_pair - top[..., None])
        total = jnp.sum(e_loc, -1) + jnp.sum(e_pair, -1)
        p_loc = e_loc / total[..., None]
        p_pair = e_pair / total[..., None]
        w_loc = p_loc.astype(bf16)
        w_pair = p_pair.astype(bf16)
        out_full = jnp.einsum("bhqk,bkhd->bqhd", w_loc, v_tile, preferred_element_type=f32)
        out_full = out_full + jnp.einsum(
            "bhqr,rbqhd->bqhd", w_pair, v_pair, preferred_element_type=f32
        )
        delta = jnp.transpose(jnp.sum(g_part.astype(f32) * out_full, -1), (0, 2, 1))
        d_loc = jnp.einsum("bqhd,bkhd->bhqk", g_part, v_tile, preferred_element_type=f32)
        d_pair = jnp.einsum("bqhd,rbqhd->bhqr", g_part, v_pair, preferred_element_type=f32)
        z_loc = (p_loc * (d_loc - delta[..., None])).astype(bf16)
        z_pair = (p_pair * (d_pair - delta[..., None])).astype(bf16)
        q_grad = jnp.einsum("bhqk,bkhd->bqhd", z_loc, k_tile, preferred_element_type=f32)
        q_grad = (
            q_grad + jnp.einsum("bhqr,rbqhd->bqhd", z_pair, k_pair, preferred_element_type=f32)
        ) * scale
        t_key = (
            jnp.einsum("bhqr,bqhd->rbqhd", z_pair, q_part, preferred_element_type=f32) * scale
        ).astype(bf16)
        t_val = jnp.einsum("bhqr,bqhd->rbqhd", w_pair, g_part, preferred_element_type=f32).astype(
            bf16
        )
        log_total = top + jnp.log(total)
        results = (
            out_full.reshape(nodes, span),
            q_grad.reshape(nodes, span),
            t_key.reshape(ROUNDS, nodes, span),
            t_val.reshape(ROUNDS, nodes, span),
            log_total,
            delta,
        )
        c_key = (
            jnp.einsum("bhqk,bqhd->bkhd", z_loc, q_part, preferred_element_type=f32) * scale
        ).reshape(blocks_dev, TMAX, BLOCK, span)
        c_val = jnp.einsum("bhqk,bqhd->bkhd", w_loc, g_part, preferred_element_type=f32).reshape(
            blocks_dev, TMAX, BLOCK, span
        )
        empty = jnp.zeros((cluster_blocks, BLOCK, span), f32)
        results = results + (
            empty.at[tiles].add(c_key).reshape(cluster_blocks * BLOCK, span),
            empty.at[tiles].add(c_val).reshape(cluster_blocks * BLOCK, span),
        )
        return results

    outputs = lax.map(head_group, jnp.arange(groups, dtype=jnp.int32))
    attended = join_heads(outputs[0]).astype(bf16)
    query_grad = join_heads(outputs[1]).astype(bf16)
    t_key = join_heads(outputs[2])
    t_val = join_heads(outputs[3])
    k_sum, v_sum = (
        lax.psum_scatter(
            settle(join_heads(outputs[6])).astype(jnp.bfloat16),
            "blk",
            scatter_dimension=0,
            tiled=True,
        ).astype(jnp.float32),
        lax.psum_scatter(
            settle(join_heads(outputs[7])).astype(jnp.bfloat16),
            "blk",
            scatter_dimension=0,
            tiled=True,
        ).astype(jnp.float32),
    )
    returned = jnp.stack(
        [
            fetch_partners(
                jnp.concatenate([t_key[step], t_val[step]], 1), partner[step], step + 1, move_terms
            )
            for step in range(ROUNDS)
        ]
    )
    returned = jnp.sum(returned.astype(f32), 0)
    key_grad = (k_sum + returned[:, :width]).astype(bf16)
    value_grad = (v_sum + returned[:, width:]).astype(bf16)
    return (attended, query_grad, key_grad, value_grad)


def solution(mesh):
    in_specs = (
        P(("grp", "blk"), None),
        P(("grp", "blk"), None),
        P(("grp", "blk"), None),
        P(("grp", "blk"), None),
        P(None, ("grp", "blk")),
        P(("grp", "blk"), None),
        P(("grp", "blk")),
    )
    out_specs = (
        P(("grp", "blk"), None),
        P(("grp", "blk"), None),
        P(("grp", "blk"), None),
        P(("grp", "blk"), None),
    )
    return jax.shard_map(shards, mesh=mesh, in_specs=in_specs, out_specs=out_specs, check_vma=False)
```

profile of v0, /device:TPU:0, one launch (start us, length us, event | category | flops | bytes accessed | tf_op | source)
XLA Modules:
  0.0 351.1 jit_solution(16281792442742700089)
XLA Ops:
  11.2 3.0 collective-permute-start.3
  14.3 1.6 collective-permute-start
  16.3 5.0 %collective-permute-done.3 = bf16[128,1024]{1,0:T(8,128)(2,1)S(1)} collective-permute-done((bf16[128,1024]{1,0:T(8,128)(2,1)S(1)}, bf16[128,1024]{1,0:T(8,128)(2,1)S(1)}, u32[]{:S(2)}, u32[]{:S(2)}) %collective-permute-start.3) | collective-permute-done | bytes 262176 | tf_op jit(solution)/shard_map/ppermute | solution.py:17
  22.2 4.8 %collective-permute-done.2 = bf16[128,1024]{1,0:T(8,128)(2,1)S(1)} collective-permute-done((bf16[128,1024]{1,0:T(8,128)(2,1)S(1)}, bf16[128,1024]{1,0:T(8,128)(2,1)S(1)}, u32[]{:S(2)}, u32[]{:S(2)}) %collective-permute-start.2) | collective-permute-done | bytes 262176 | tf_op jit(solution)/shard_map/ppermute | solution.py:17
  28.7 2.3 collective-permute-done
  33.5 52.7 %all-gather.2.cloned.1.call-done = bf16[2048,1024]{1,0:T(8,128)(2,1)} async-done(((bf16[256,1024]{1,0:T(8,128)(2,1)}), bf16[2048,1024]{1,0:T(8,128)(2,1)}) %all-gather.2.cloned.1.call-update) | async-done | bytes 4194320 | tf_op jit(solution)/shard_map/all_gather | solution.py:58
  86.3 2.9 gather_fusion
  89.2 4.8 %copy.120 = bf16[2,6,128,1024]{2,1,3,0:T(8,128)(2,1)} copy(bf16[2,6,128,1024]{3,2,1,0:T(8,128)(2,1)S(1)} %bitcast.194) | data formatting | bytes 6291456
  94.7 108.1 %while.23 = (s32[]{:T(128)}, bf16[4,256,128]{1,2,0:T(8,128)(2,1)}, bf16[4,256,128]{1,2,0:T(8,128)(2,1)}, bf16[4,2,256,128]{2,3,1,0:T(8,128)(2,1)}, bf16[4,2,256,...) while((s32[]{:T(128)}, bf16[4,256,128]{1,2,0:T(8,128)(2,1)}, ...), condition=%wide.region_8.9_spmd.clone, body=%wide.region_0.8_spmd.clone.sunk | while | flops 309147168 | bytes 47453524 | solution.py:138
  106.4 1.6 multiply_convert_fusion.6
  115.8 2.4 copy.241
  133.4 1.6 multiply_convert_fusion.6
  142.9 2.4 copy.241
  160.4 1.6 multiply_convert_fusion.6
  169.9 2.4 copy.241
  187.5 1.6 multiply_convert_fusion.6
  196.9 2.4 copy.241
  202.8 3.1 copy_bitcast_fusion.1
  213.1 1.7 collective-permute-start.4
  216.5 3.4 collective-permute-done.7
  220.9 4.6 %collective-permute-done.6 = bf16[128,1024]{1,0:T(8,128)(2,1)S(1)} collective-permute-done((bf16[128,1024]{1,0:T(8,128)(2,1)S(1)}, bf16[128,1024]{1,0:T(8,128)(2,1)S(1)}, u32[]{:S(2)}, u32[]{:S(2)}) %collective-permute-start.6) | collective-permute-done | bytes 262176 | tf_op jit(solution)/shard_map/ppermute | solution.py:17
  229.0 43.1 %reduce-scatter.5.cloned.1.call-done = bf16[256,512]{1,0:T(8,128)(2,1)} async-done(((bf16[2048,512]{1,0:T(8,128)(2,1)}), bf16[256,512]{1,0:T(8,128)(2,1)}) %reduce-scatter.5.cloned.1.call-update) | async-done | bytes 262160 | tf_op jit(solution)/shard_map/reduce_scatter | solution.py:150
  272.1 70.5 %reduce-scatter.3.cloned.1.call-done = bf16[256,512]{1,0:T(8,128)(2,1)} async-done(((bf16[2048,512]{1,0:T(8,128)(2,1)}), bf16[256,512]{1,0:T(8,128)(2,1)}) %reduce-scatter.3.cloned.1.call-update) | async-done | bytes 262160 | tf_op jit(solution)/shard_map/reduce_scatter | solution.py:144
  342.6 2.0 fusion.16
  (447 shorter events, 110.6 us)
Async XLA Ops:
  7.2 8.8 %copy-start.18 = (s32[2,6]{1,0:T(2,128)S(1)}, s32[2,6]{1,0:T(2,128)}, u32[]{:S(2)}) copy-start(s32[2,6]{1,0:T(2,128)} %param.14) | copy-start | bytes 148
  7.2 8.9 %copy-start.26 = (s32[2,256]{1,0:T(2,128)S(1)}, s32[2,256]{1,0:T(2,128)}, u32[]{:S(2)}) copy-start(s32[2,256]{1,0:T(2,128)} %param.13) | copy-start | bytes 6148
  7.2 9.0 %copy-start.27 = (s32[2]{0:T(128)S(1)}, s32[2]{0:T(128)}, u32[]{:S(2)}) copy-start(s32[2]{0:T(128)} %param.15) | copy-start | bytes 28
  7.2 79.1 %all-gather.2.cloned.1.call-start = ((), (), s32[]{:S(2)}) async-start(), calls=%async_computation.2 | async-start | bytes 4718592 | tf_op jit(solution)/shard_map/all_gather | solution.py:58
  10.0 262.1 %reduce-scatter.5.cloned.1.call-start = ((), (), s32[]{:S(2)}) async-start(), calls=%async_computation.4 | async-start | bytes 2359296 | tf_op jit(solution)/shard_map/reduce_scatter | solution.py:150
  11.2 10.1 %collective-permute-start.3 = (bf16[128,1024]{1,0:T(8,128)(2,1)S(1)}, bf16[128,1024]{1,0:T(8,128)(2,1)S(1)}, u32[]{:S(2)}, u32[]{:S(2)}) collective-permute-start(bf16[128,1024]{1,0:T(8,128)(2,1)S(1)} %get-tuple-element.334), channel_id=1, source_target_pairs={{0,16},{8,24},{16,0},{24,8},{1,17},{9,25},{17,1},{25,9},{2,18},{10... | collective-permute-start | bytes 786440 | tf_op jit(solution)/shard_map/ppermute | solution.py:17
  14.2 13.6 %collective-permute-start.1 = (bf16[128,1024]{1,0:T(8,128)(2,1)S(1)}, bf16[128,1024]{1,0:T(8,128)(2,1)S(1)}, u32[]{:S(2)}, u32[]{:S(2)}) collective-permute-start(bf16[128,1024]{1,0:T(8,128)(2,1)S(1)} %get-tuple-element.334), channel_id=1, source_target_pairs={{0,8},{8,16},{16,24},{24,0},{1,9},{9,17},{17,25},{25,1},{2,10},{10... | collective-permute-start | bytes 786440 | tf_op jit(solution)/shard_map/ppermute | solution.py:17
  14.2 12.7 %collective-permute-start.2 = (bf16[128,1024]{1,0:T(8,128)(2,1)S(1)}, bf16[128,1024]{1,0:T(8,128)(2,1)S(1)}, u32[]{:S(2)}, u32[]{:S(2)}) collective-permute-start(bf16[128,1024]{1,0:T(8,128)(2,1)S(1)} %get-tuple-element.333), channel_id=1, source_target_pairs={{0,16},{8,24},{16,0},{24,8},{1,17},{9,25},{17,1},{25,9},{2,18},{10... | collective-permute-start | bytes 786440 | tf_op jit(solution)/shard_map/ppermute | solution.py:17
  14.3 16.6 %collective-permute-start = (bf16[128,1024]{1,0:T(8,128)(2,1)S(1)}, bf16[128,1024]{1,0:T(8,128)(2,1)S(1)}, u32[]{:S(2)}, u32[]{:S(2)}) collective-permute-start(bf16[128,1024]{1,0:T(8,128)(2,1)S(1)} %get-tuple-element.333), channel_id=1, source_target_pairs={{0,24},{8,0},{16,8},{24,16},{1,25},{9,1},{17,9},{25,17},{2,26},{10... | collective-permute-start | bytes 786440 | tf_op jit(solution)/shard_map/ppermute | solution.py:17
  16.1 11.7 %copy-start.24 = (s32[1024]{0:T(1024)}, s32[1024]{0:T(1024)S(1)}, u32[]{:S(2)}) copy-start(s32[1024]{0:T(1024)S(1)} %get-tuple-element.340) | copy-start | bytes 12292
  16.1 11.7 %copy-start.25 = (s32[1024]{0:T(1024)}, s32[1024]{0:T(1024)S(1)}, u32[]{:S(2)}) copy-start(s32[1024]{0:T(1024)S(1)} %get-tuple-element.339) | copy-start | bytes 12292
  16.1 11.7 %copy-start.23 = (s32[1024]{0:T(1024)}, s32[1024]{0:T(1024)S(1)}, u32[]{:S(2)}) copy-start(s32[1024]{0:T(1024)S(1)} %get-tuple-element.341) | copy-start | bytes 12292
  16.1 14.9 %copy-start.22 = (s32[1024]{0:T(1024)}, s32[1024]{0:T(1024)S(1)}, u32[]{:S(2)}) copy-start(s32[1024]{0:T(1024)S(1)} %get-tuple-element.342) | copy-start | bytes 12292
  98.9 7.4 %copy-start.3 = (bf16[2,768,2,64]{1,3,2,0:T(8,128)(2,1)}, bf16[2,768,2,64]{1,3,2,0:T(8,128)(2,1)S(1)}, u32[]{:S(2)}) copy-start(bf16[2,768,2,64]{1,3,2,0:T(8,128)(2,1)S(1)} %reshape.399) | copy-start | bytes 1179652 | tf_op jit(solution)/shard_map/while
  121.7 6.4 %copy-start.20 = (pred[2,6]{1,0:T(4,128)(4,1)}, pred[2,6]{1,0:T(4,128)(4,1)S(1)}, u32[]{:S(2)}) copy-start(pred[2,6]{1,0:T(4,128)(4,1)S(1)} %get-tuple-element.525) | copy-start | bytes 40 | tf_op jit(solution)/shard_map/while
  126.0 7.4 %copy-start.3 = (bf16[2,768,2,64]{1,3,2,0:T(8,128)(2,1)}, bf16[2,768,2,64]{1,3,2,0:T(8,128)(2,1)S(1)}, u32[]{:S(2)}) copy-start(bf16[2,768,2,64]{1,3,2,0:T(8,128)(2,1)S(1)} %reshape.399) | copy-start | bytes 1179652 | tf_op jit(solution)/shard_map/while
  148.7 6.4 %copy-start.20 = (pred[2,6]{1,0:T(4,128)(4,1)}, pred[2,6]{1,0:T(4,128)(4,1)S(1)}, u32[]{:S(2)}) copy-start(pred[2,6]{1,0:T(4,128)(4,1)S(1)} %get-tuple-element.525) | copy-start | bytes 40 | tf_op jit(solution)/shard_map/while
  153.0 7.4 %copy-start.3 = (bf16[2,768,2,64]{1,3,2,0:T(8,128)(2,1)}, bf16[2,768,2,64]{1,3,2,0:T(8,128)(2,1)S(1)}, u32[]{:S(2)}) copy-start(bf16[2,768,2,64]{1,3,2,0:T(8,128)(2,1)S(1)} %reshape.399) | copy-start | bytes 1179652 | tf_op jit(solution)/shard_map/while
  180.0 7.4 %copy-start.3 = (bf16[2,768,2,64]{1,3,2,0:T(8,128)(2,1)}, bf16[2,768,2,64]{1,3,2,0:T(8,128)(2,1)S(1)}, u32[]{:S(2)}) copy-start(bf16[2,768,2,64]{1,3,2,0:T(8,128)(2,1)S(1)} %reshape.399) | copy-start | bytes 1179652 | tf_op jit(solution)/shard_map/while
  206.0 136.7 %reduce-scatter.3.cloned.1.call-start = ((), (), s32[]{:S(2)}) async-start(), calls=%async_computation.3 | async-start | bytes 2359296 | tf_op jit(solution)/shard_map/reduce_scatter | solution.py:144
  210.6 9.3 %collective-permute-start.7 = (bf16[128,1024]{1,0:T(8,128)(2,1)S(1)}, bf16[128,1024]{1,0:T(8,128)(2,1)S(1)}, u32[]{:S(2)}, u32[]{:S(2)}) collective-permute-start(bf16[128,1024]{1,0:T(8,128)(2,1)S(1)} %get-tuple-element.332), channel_id=1, source_target_pairs={{0,16},{8,24},{16,0},{24,8},{1,17},{9,25},{17,1},{25,9},{2,18},{10... | collective-permute-start | bytes 786440 | tf_op jit(solution)/shard_map/ppermute | solution.py:17
  212.1 13.4 %collective-permute-start.6 = (bf16[128,1024]{1,0:T(8,128)(2,1)S(1)}, bf16[128,1024]{1,0:T(8,128)(2,1)S(1)}, u32[]{:S(2)}, u32[]{:S(2)}) collective-permute-start(bf16[128,1024]{1,0:T(8,128)(2,1)S(1)} %get-tuple-element.331), channel_id=1, source_target_pairs={{0,16},{8,24},{16,0},{24,8},{1,17},{9,25},{17,1},{25,9},{2,18},{10... | collective-permute-start | bytes 786440 | tf_op jit(solution)/shard_map/ppermute | solution.py:17
  213.0 13.5 %collective-permute-start.5 = (bf16[128,1024]{1,0:T(8,128)(2,1)S(1)}, bf16[128,1024]{1,0:T(8,128)(2,1)S(1)}, u32[]{:S(2)}, u32[]{:S(2)}) collective-permute-start(bf16[128,1024]{1,0:T(8,128)(2,1)S(1)} %get-tuple-element.326), channel_id=1, source_target_pairs={{0,8},{8,16},{16,24},{24,0},{1,9},{9,17},{17,25},{25,1},{2,10},{10... | collective-permute-start | bytes 786440 | tf_op jit(solution)/shard_map/ppermute | solution.py:17
  213.1 14.6 %collective-permute-start.4 = (bf16[128,1024]{1,0:T(8,128)(2,1)S(1)}, bf16[128,1024]{1,0:T(8,128)(2,1)S(1)}, u32[]{:S(2)}, u32[]{:S(2)}) collective-permute-start(bf16[128,1024]{1,0:T(8,128)(2,1)S(1)} %get-tuple-element.325), channel_id=1, source_target_pairs={{0,24},{8,0},{16,8},{24,16},{1,25},{9,1},{17,9},{25,17},{2,26},{10... | collective-permute-start | bytes 786440 | tf_op jit(solution)/shard_map/ppermute | solution.py:17
  (60 other events, 129.6 us)
Sparse Core Ops, SparseCore 0:
  10.2 76.0 all-gather.1
  206.1 65.9 reduce-scatter.4
  275.7 66.9 reduce-scatter.2
where the time goes:
time: 352 us; the launch traced here: 351 us
  waiting for transfers between devices  187 us (53%)
  local copies, waits for them, and re-layouts  93.5 us (27%)
  other arithmetic  23.4 us (7%)
  matrix products  19.7 us (6%)
  between operations  14.1 us (4%)
  starting transfers between devices  9 us (3%)
  loops' own time  4.64 us (1%)
    reduce_scatter x1, waiting for transfers between devices, shards(): lax.psum_scatter(settle(join_heads(outputs[6])).astype(jnp.bfloat16), 'bl...  70.5 us
    all_gather x1, waiting for transfers between devices, shards(): cluster_rows = lax.all_gather(both, 'blk', axis=0, tiled=True)  52.7 us
    reduce_scatter x1, waiting for transfers between devices, shards(): lax.psum_scatter(settle(join_heads(outputs[7])).astype(jnp.bfloat16), 'bl...  43.1 us
    ppermute x8, waiting for transfers between devices, passed_along(): return lax.ppermute(x, axis, [(i, (i + by) % size) for i in range(size)])  20.3 us
    reshape x8, local copies, waits for them, and re-layouts, head_group(): c_key = (jnp.einsum('bhqk,bqhd->bkhd', z_loc, q_part, preferred_element_t...  13 us
    unnamed x29, local copies, waits for them, and re-layouts  10.5 us
    dynamic_update_slice x12, local copies, waits for them, and re-layouts, shards(): outputs = lax.map(head_group, jnp.arange(groups, dtype=jnp.int32))  10.1 us
    ppermute x8, starting transfers between devices, passed_along(): return lax.ppermute(x, axis, [(i, (i + by) % size) for i in range(size)])  8.66 us
  transfers between devices with their start and end apart: 11, of which 9 were waited for; matrix products, arithmetic and copies ran while one was open for 4% of the time, Pallas kernels for 0%

commit v1 on v0

v1 whole, which is shorter than its diff:
```python
import functools

import jax
import jax.numpy as jnp
from jax import lax
from jax.experimental import pallas as pl
from jax.experimental.pallas import tpu as pltpu
from jax.sharding import PartitionSpec as P

HEADS = 8
HEAD_DIM = 64
BLOCK = 128
TMAX = 6
ROUNDS = 2
NEG_BIG = -1e30
SCALE = HEAD_DIM**-0.5
MESH = pl.DeviceIdType.MESH
VMEM = pltpu.VMEM
F32 = jnp.float32
BF16 = jnp.bfloat16
LIMIT = 40 * 1024 * 1024


def grp_offsets(clusters):
    found = set()
    for step in range(ROUNDS):
        found.add((step + 1) % clusters)
        found.add((-step - 1) % clusters)
    return sorted(found - {0})


def greet(clusters, team, row, me):
    barrier = pltpu.get_barrier_semaphore()
    offsets = grp_offsets(clusters)
    for offset in offsets:
        pl.semaphore_signal(
            barrier,
            inc=1,
            device_id=(lax.rem(row + offset, clusters), me),
            device_id_type=MESH,
        )
    for offset in range(1, team):
        pl.semaphore_signal(
            barrier, inc=1, device_id=(row, lax.rem(me + offset, team)), device_id_type=MESH
        )
    return barrier, len(offsets) + team - 1


def remote(src, dst, send_sem, recv_sem, target):
    return pltpu.make_async_remote_copy(
        src_ref=src,
        dst_ref=dst,
        send_sem=send_sem,
        recv_sem=recv_sem,
        device_id=target,
        device_id_type=MESH,
    )


def head_marks(rows, slot, width):
    at = lax.broadcasted_iota(jnp.int32, (rows, width), 0)
    column = lax.broadcasted_iota(jnp.int32, (rows, width), 1)
    hit = at == (column // HEAD_DIM) * 8 + slot
    return jnp.where(hit, 1.0, 0.0).astype(BF16)


def pick_rows(slots):
    at = lax.broadcasted_iota(jnp.int32, (BLOCK, BLOCK), 0)
    hit = jnp.where(at == jnp.broadcast_to(slots, (BLOCK, BLOCK)), 1.0, 0.0)
    return hit.T.astype(BF16)


def dot_last(left, right):
    return lax.dot_general(left, right, (((1,), (1,)), ((), ())), preferred_element_type=F32)


def dot(left, right):
    return jnp.dot(left, right, preferred_element_type=F32)


def spread_kernel(
    clusters,
    team,
    q_ref,
    k_ref,
    v_ref,
    g_ref,
    partner_ref,
    meta_ref,
    x_ref,
    pair_ref,
    meta_all_ref,
    kp_ref,
    vp_ref,
    packed,
    pair_out,
    kbuf,
    vbuf,
    x_send,
    x_recv,
    p_send,
    p_recv,
    m_send,
    m_recv,
    g_send,
    g_recv,
):
    row = lax.axis_index("grp")
    me = lax.axis_index("blk")
    width = q_ref.shape[1]
    barrier, count = greet(clusters, team, row, me)

    for head in range(team):
        left = head * HEAD_DIM
        for half in range(2):
            rows = slice(half * BLOCK, (half + 1) * BLOCK)
            cols = slice(left, left + HEAD_DIM)
            packed[head, half] = jnp.concatenate([q_ref[rows, cols], g_ref[rows, cols]], 1)
            packed[head, 2 + half] = jnp.concatenate([k_ref[rows, cols], v_ref[rows, cols]], 1)

    pl.semaphore_wait(barrier, count)

    moves = []
    for step in range(ROUNDS):
        by = step + 1
        ahead = (lax.rem(row + by, clusters), me)
        behind = (lax.rem(row + clusters - by, clusters), me)
        for at, (src, dst) in enumerate(((k_ref, kbuf), (v_ref, vbuf))):
            for half, target in ((0, behind), (1, ahead)):
                rows = pl.ds((1 - half) * BLOCK, BLOCK)
                index = (step * 2 + at) * 2 + half
                copy = remote(
                    src.at[rows], dst.at[step, half], g_send.at[index], g_recv.at[index], target
                )
                copy.start()
                moves.append(copy)

    sends = []
    for offset in range(1, team):
        peer = lax.rem(me + offset, team)
        target = (row, peer)
        copy = remote(
            meta_ref, meta_all_ref.at[me], m_send.at[offset], m_recv.at[offset], target
        )
        copy.start()
        sends.append(copy)
    for offset in range(1, team):
        peer = lax.rem(me + offset, team)
        target = (row, peer)
        copy = remote(packed.at[peer], x_ref.at[me], x_send.at[offset], x_recv.at[offset], target)
        copy.start()
        sends.append(copy)
    x_ref[me] = packed[me]
    meta_all_ref[me] = meta_ref[...]

    for copy in moves:
        copy.wait()
    marks = [head_marks(8 * HEADS, slot, width) for slot in range(2 * ROUNDS)]
    for half in range(2):
        rows = slice(half * BLOCK, (half + 1) * BLOCK)
        total = None
        for step in range(ROUNDS):
            pick = pick_rows(partner_ref[step : step + 1, rows])
            for at, (buf, out, near) in enumerate(
                ((kbuf, kp_ref, q_ref), (vbuf, vp_ref, g_ref))
            ):
                taken = dot(pick, buf[step, half])
                out[step, rows] = taken.astype(BF16)
                product = near[rows].astype(F32) * taken
                high = product.astype(BF16)
                low = (product - high.astype(F32)).astype(BF16)
                mark = marks[at * ROUNDS + step]
                part = dot_last(mark, high) + dot_last(mark, low)
                total = part if total is None else total + part
        pair_out[:, half] = total.reshape(HEADS, 8, BLOCK)
    for offset in range(1, team):
        peer = lax.rem(me + offset, team)
        copy = remote(
            pair_out.at[peer], pair_ref.at[me], p_send.at[offset], p_recv.at[offset], (row, peer)
        )
        copy.start()
        sends.append(copy)
    pair_ref[me] = pair_out[me]
    for copy in sends:
        copy.wait()


def attend_kernel(x_ref, pair_ref, meta_ref, y_ref, pw_ref, kvt, acc):
    team = x_ref.shape[0]
    blocks = 2 * team
    lane = lax.broadcasted_iota(jnp.int32, (BLOCK, BLOCK), 1) < HEAD_DIM
    for unit in range(team):
        for half in range(2):
            kvt[2 * unit + half] = x_ref[unit, 2 + half].astype(F32).T.astype(BF16)
    acc[...] = jnp.zeros_like(acc)

    def body(block, carry):
        unit = block // 2
        half = block % 2
        qg = x_ref[unit, half].astype(F32)
        qg2 = jnp.concatenate([jnp.where(lane, qg, 0.0), jnp.where(lane, 0.0, qg)], 0).astype(BF16)
        ids = [meta_ref[unit, half, slot] for slot in range(TMAX)]
        live = meta_ref[unit, half, TMAX]
        pair = pair_ref[unit, half]
        s_pair = [pair[r : r + 1] * SCALE for r in range(ROUNDS)]
        d_pair = [pair[ROUNDS + r : ROUNDS + r + 1] for r in range(ROUNDS)]
        s_loc, d_loc = [], []
        top = functools.reduce(jnp.maximum, s_pair)
        for slot in range(TMAX):
            kv = x_ref[ids[slot] // 2, 2 + ids[slot] % 2]
            both = dot_last(kv, qg2)
            scores = both[:, :BLOCK] * SCALE + jnp.where(slot < live, 0.0, NEG_BIG)
            s_loc.append(scores)
            d_loc.append(both[:, BLOCK:])
            top = jnp.maximum(top, jnp.max(scores, 0, keepdims=True))
        e_pair = [jnp.exp(s - top) for s in s_pair]
        total = functools.reduce(jnp.add, e_pair)
        e_loc = []
        for slot in range(TMAX):
            e = jnp.exp(s_loc[slot] - top)
            e_loc.append(e)
            total = total + jnp.sum(e, 0, keepdims=True)
        inverse = 1.0 / total
        p_pair = [e * inverse for e in e_pair]
        w_pair = [p.astype(BF16).astype(F32) for p in p_pair]
        delta = functools.reduce(jnp.add, [w * d for w, d in zip(w_pair, d_pair)])
        p_loc, w_loc = [], []
        for slot in range(TMAX):
            p = e_loc[slot] * inverse
            w = p.astype(BF16)
            p_loc.append(p)
            w_loc.append(w)
            delta = delta + jnp.sum(w.astype(F32) * d_loc[slot], 0, keepdims=True)
        z_pair = [(p * (d - delta)).astype(BF16).astype(F32) for p, d in zip(p_pair, d_pair)]
        pw_ref[unit, half] = jnp.concatenate(
            w_pair + z_pair + [jnp.zeros((8 - 2 * ROUNDS, BLOCK), F32)], 0
        )
        back = None
        for slot in range(TMAX):
            z = (p_loc[slot] * (d_loc[slot] - delta)).astype(BF16)
            zw = jnp.concatenate([z, w_loc[slot]], 1)
            acc[ids[slot]] += dot(zw, qg2)
            part = dot(kvt[ids[slot]], zw)
            back = part if back is None else back + part
        turned = jnp.concatenate([back[:HEAD_DIM, :BLOCK] * SCALE, back[HEAD_DIM:, BLOCK:]], 0)
        y_ref[unit, half] = turned.T.astype(BF16)
        return carry

    lax.fori_loop(0, blocks, body, 0, unroll=2)
    for unit in range(team):
        for half in range(2):
            grads = acc[2 * unit + half]
            y_ref[unit, 2 + half] = jnp.where(lane, grads * SCALE, grads).astype(BF16)


def collect_kernel(
    clusters,
    team,
    y_ref,
    pw_ref,
    q_ref,
    g_ref,
    kp_ref,
    vp_ref,
    partner_ref,
    out_ref,
    dq_ref,
    dk_ref,
    dv_ref,
    ybuf,
    pbuf,
    terms,
    tbuf,
    y_send,
    y_recv,
    p_send,
    p_recv,
    g_send,
    g_recv,
):
    row = lax.axis_index("grp")
    me = lax.axis_index("blk")
    width = q_ref.shape[1]
    barrier, count = greet(clusters, team, row, me)
    pl.semaphore_wait(barrier, count)
    small, large = [], []
    for offset in range(1, team):
        peer = lax.rem(me + offset, team)
        copy = remote(
            pw_ref.at[peer], pbuf.at[me], p_send.at[offset], p_recv.at[offset], (row, peer)
        )
        copy.start()
        small.append(copy)
    for offset in range(1, team):
        peer = lax.rem(me + offset, team)
        copy = remote(
            y_ref.at[peer], ybuf.at[me], y_send.at[offset], y_recv.at[offset], (row, peer)
        )
        copy.start()
        large.append(copy)
    pbuf[me] = pw_ref[me]
    ybuf[me] = y_ref[me]
    for copy in small:
        copy.wait()

    marks = [head_marks(BLOCK, slot, width) for slot in range(2 * ROUNDS)]
    moves = []
    for half in range(2):
        rows = slice(half * BLOCK, (half + 1) * BLOCK)
        flat = pbuf[:, half].reshape(8 * HEADS, BLOCK)
        flat = jnp.concatenate([flat, jnp.zeros((BLOCK - 8 * HEADS, BLOCK), F32)], 0)
        turned = flat.T.astype(BF16)
        out_add = None
        dq_add = None
        for step in range(ROUNDS):
            by = step + 1
            w = dot(turned, marks[step])
            z = dot(turned, marks[ROUNDS + step]) * SCALE
            terms[step, half, :, :width] = (z * q_ref[rows].astype(F32)).astype(BF16)
            terms[step, half, :, width:] = (w * g_ref[rows].astype(F32)).astype(BF16)
            shift = by if half == 0 else clusters - by
            target = (lax.rem(row + shift, clusters), me)
            index = step * 2 + half
            copy = remote(
                terms.at[step, half],
                tbuf.at[step, 1 - half],
                g_send.at[index],
                g_recv.at[index],
                target,
            )
            copy.start()
            moves.append(copy)
            out_part = w * vp_ref[step, rows].astype(F32)
            dq_part = z * kp_ref[step, rows].astype(F32)
            out_add = out_part if out_add is None else out_add + out_part
            dq_add = dq_part if dq_add is None else dq_add + dq_part
        out_hold = out_add
        dq_hold = dq_add
        dv_ref[rows] = out_hold.astype(BF16)
        dk_ref[rows] = dq_hold.astype(BF16)

    for copy in large:
        copy.wait()

    def heads_of(half, left):
        parts = [ybuf[head, half][:, left : left + HEAD_DIM] for head in range(team)]
        return jnp.concatenate(parts, 1).astype(F32)

    for half in range(2):
        rows = slice(half * BLOCK, (half + 1) * BLOCK)
        dq_ref[rows] = (heads_of(half, 0) + dk_ref[rows].astype(F32)).astype(BF16)
        out_ref[rows] = (heads_of(half, HEAD_DIM) + dv_ref[rows].astype(F32)).astype(BF16)

    for copy in moves:
        copy.wait()
    for half in range(2):
        rows = slice(half * BLOCK, (half + 1) * BLOCK)
        back = None
        for step in range(ROUNDS):
            pick = pick_rows(partner_ref[step : step + 1, rows])
            part = dot(pick, tbuf[step, half])
            back = part if back is None else back + part
        dk_ref[rows] = (heads_of(2 + half, 0) + back[:, :width]).astype(BF16)
        dv_ref[rows] = (heads_of(2 + half, HEAD_DIM) + back[:, width:]).astype(BF16)


def shards(clusters, team, query, key, value, out_grad, partner, tiles, tile_count):
    nodes, width = query.shape
    meta = jnp.concatenate([tiles, tile_count[:, None]], 1)
    meta = jnp.pad(meta, ((0, 8 - meta.shape[0]), (0, 128 - meta.shape[1])))
    shape = jax.ShapeDtypeStruct
    whole = pl.BlockSpec(memory_space=VMEM)
    dma = pltpu.SemaphoreType.DMA
    big = (team, 4, BLOCK, BLOCK)
    few = (team, 2, 8, BLOCK)
    x, pair, meta_all, kp, vp = pl.pallas_call(
        functools.partial(spread_kernel, clusters, team),
        out_shape=(
            shape(big, BF16),
            shape(few, F32),
            shape((team, 8, 128), jnp.int32),
            shape((ROUNDS, nodes, width), BF16),
            shape((ROUNDS, nodes, width), BF16),
        ),
        in_specs=[whole] * 6,
        out_specs=(whole,) * 5,
        scratch_shapes=[
            VMEM(big, BF16),
            VMEM(few, F32),
            VMEM((ROUNDS, 2, BLOCK, width), BF16),
            VMEM((ROUNDS, 2, BLOCK, width), BF16),
        ]
        + [dma((team,))] * 6
        + [dma((4 * ROUNDS,))] * 2,
        compiler_params=pltpu.CompilerParams(
            collective_id=0, has_side_effects=True, vmem_limit_bytes=LIMIT
        ),
    )(query, key, value, out_grad, partner, meta)
    y, pw = pl.pallas_call(
        attend_kernel,
        out_shape=(shape(big, BF16), shape(few, F32)),
        in_specs=[whole, whole, pl.BlockSpec(memory_space=pltpu.SMEM)],
        out_specs=(whole, whole),
        scratch_shapes=[
            VMEM((2 * team, BLOCK, BLOCK), BF16),
            VMEM((2 * team, BLOCK, BLOCK), F32),
        ],
        compiler_params=pltpu.CompilerParams(vmem_limit_bytes=LIMIT),
    )(x, pair, meta_all)
    return pl.pallas_call(
        functools.partial(collect_kernel, clusters, team),
        out_shape=(shape((nodes, width), BF16),) * 4,
        in_specs=[whole] * 7,
        out_specs=(whole,) * 4,
        scratch_shapes=[
            VMEM(big, BF16),
            VMEM(few, F32),
            VMEM((ROUNDS, 2, BLOCK, 2 * width), BF16),
            VMEM((ROUNDS, 2, BLOCK, 2 * width), BF16),
        ]
        + [dma((team,))] * 4
        + [dma((2 * ROUNDS,))] * 2,
        compiler_params=pltpu.CompilerParams(
            collective_id=1, has_side_effects=True, vmem_limit_bytes=LIMIT
        ),
    )(y, pw, query, out_grad, kp, vp, partner)


def solution(mesh):
    rows = P(("grp", "blk"), None)
    in_specs = (rows, rows, rows, rows, P(None, ("grp", "blk")), rows, P(("grp", "blk")))
    return jax.shard_map(
        functools.partial(shards, mesh.shape["grp"], mesh.shape["blk"]),
        mesh=mesh,
        in_specs=in_specs,
        out_specs=(rows,) * 4,
        check_vma=False,
    )
```

time: 352 us -> 84.8 us (0.24)
  waiting for transfers between devices: 187 us -> 0 us
  local copies, waits for them, and re-layouts: 93.5 us -> 8.62 us
  Pallas kernels: 0 us -> 75.2 us
  other arithmetic: 23.4 us -> 0.07 us
  matrix products: 19.7 us -> 0 us
  between operations: 14.1 us -> 0.69 us
  starting transfers between devices: 9 us -> 0 us
  loops' own time: 4.64 us -> 0 us
    reduce_scatter x2 -> x0, waiting for transfers between devices: 114 us -> none  [the longest x1 70.5 us: shards(): lax.psum_scatter(settle(join_heads(outputs[6])).astype(jnp.bfloat16), 'bl...]
    pallas_call x0 -> x3, Pallas kernels: none -> 75.2 us  [the longest x1 32.4 us: shards(): pl.pallas_call(functools.partial(spread_kernel, clusters, team), out_shap...]
    all_gather x1 -> x0, waiting for transfers between devices: 52.7 us -> none  [shards(): cluster_rows = lax.all_gather(both, 'blk', axis=0, tiled=True)]
    reshape x40 -> x0, local copies, waits for them, and re-layouts: 23.9 us -> none  [the longest x8 13 us: head_group(): c_key = (jnp.einsum('bhqk,bqhd->bkhd', z_loc, q_part, preferred_element_t...]
    dynamic_slice x28 -> x0, local copies, waits for them, and re-layouts: 22.7 us -> none  [the longest x4 5.58 us: head_group(): lax.dynamic_slice_in_dim(tiled, left, span, 3)]
    ppermute x8 -> x0, waiting for transfers between devices: 20.3 us -> none  [passed_along(): return lax.ppermute(x, axis, [(i, (i + by) % size) for i in range(size)])]
    dot_general x24 -> x0, matrix products: 19.7 us -> none  [the longest x4 6.53 us: head_group(): jnp.einsum('bqhd,bkhd->bhqk', g_part, v_tile, preferred_element_type=f32)]
    scatter-add x8 -> x0, other arithmetic: 11.1 us -> none  [the longest x4 5.55 us: head_group(): empty.at[tiles].add(c_val).reshape(cluster_blocks * BLOCK, span)]
  transfers between devices with their start and end apart: 11 -> 0, of which waited for: 9 -> 0; matrix products, arithmetic and copies ran while one was open for 4% -> 0% of each run, Pallas kernels for 0% -> 0%
where the time goes in v1:
time: 84.8 us; the launch traced here: 84.5 us
  Pallas kernels  75.2 us (89%)
  local copies, waits for them, and re-layouts  8.62 us (10%)
    pallas_call x1, Pallas kernels, shards(): pl.pallas_call(functools.partial(spread_kernel, clusters, team), out_shap...  32.4 us
    pallas_call x1, Pallas kernels, shards(): pl.pallas_call(functools.partial(collect_kernel, clusters, team), out_sha...  28.5 us
    pallas_call x1, Pallas kernels, shards(): pl.pallas_call(attend_kernel, out_shape=(shape(big, BF16), shape(few, F32...  14.3 us
    unnamed x20, local copies, waits for them, and re-layouts  8.52 us

profile of v1, /device:TPU:0, one launch (start us, length us, event | category | flops | bytes accessed | tf_op | source)
XLA Modules:
  0.0 84.5 jit_solution(14456883802008020492)
XLA Ops:
  0.6 0.0 copy-start.7
  0.6 0.6 copy-done.7
  1.3 0.0 copy-start.6
  1.3 0.1 copy.11
  1.4 0.6 copy-done.6
  2.0 0.1 pad_add_fusion
  2.0 0.0 copy-start.5
  2.0 0.7 copy-done.5
  2.7 0.0 copy-start
  2.7 0.9 %copy-done = bf16[256,512]{1,0:T(8,128)(2,1)S(1)} copy-done((bf16[256,512]{1,0:T(8,128)(2,1)S(1)}, bf16[256,512]{1,0:T(8,128)(2,1)}, u32[]{:S(2)}) %copy-start) | copy-done | bytes 262168
  3.7 0.0 copy-start.1
  3.7 0.9 %copy-done.1 = bf16[256,512]{1,0:T(8,128)(2,1)S(1)} copy-done((bf16[256,512]{1,0:T(8,128)(2,1)S(1)}, bf16[256,512]{1,0:T(8,128)(2,1)}, u32[]{:S(2)}) %copy-start.1) | copy-done | bytes 262168
  4.6 0.0 copy-start.3
  4.6 0.9 %copy-done.3 = bf16[256,512]{1,0:T(8,128)(2,1)S(1)} copy-done((bf16[256,512]{1,0:T(8,128)(2,1)S(1)}, bf16[256,512]{1,0:T(8,128)(2,1)}, u32[]{:S(2)}) %copy-start.3) | copy-done | bytes 262168
  5.6 0.9 %copy-done.4 = bf16[256,512]{1,0:T(8,128)(2,1)S(1)} copy-done((bf16[256,512]{1,0:T(8,128)(2,1)S(1)}, bf16[256,512]{1,0:T(8,128)(2,1)}, u32[]{:S(2)}) %copy-start.4) | copy-done | bytes 262168
  6.5 32.4 %shard_map.102 = (bf16[8,4,128,128]{3,2,1,0:T(8,128)(2,1)S(1)}, f32[8,2,8,128]{3,2,1,0:T(8,128)S(1)}, s32[8,8,128]{2,1,0:T(8,128)S(1)}, bf16[2,256,512]{2,1,0:T(8,128)(2,1)S(1)}, bf16[2,256,512]{2,1,0:T(8,128)(2,1)S(1)}) custom-call(bf16[256,512]{1,0:T(8,128)(2,1)S(1)} %copy-done, bf16[256,512]{1,0:T(8,128)(2,1)S(1)} %copy-done.3, ...), custom_call_target="tpu_custom_call" | custom-call | tf_op jit(solution)/shard_map/pallas_call | solution.py:376
  38.9 0.0 copy-start.2
  38.9 14.3 %shard_map.103 = (bf16[8,4,128,128]{3,2,1,0:T(8,128)(2,1)S(1)}, f32[8,2,8,128]{3,2,1,0:T(8,128)S(1)}) custom-call(bf16[8,4,128,128]{3,2,1,0:T(8,128)(2,1)S(1)} %get-tuple-element.11.x_ref, f32[8,2,8,128]{3,2,1,0:T(8,128)S(1)} %get-tuple-element.12.pair_ref, s32[8,8,128]{2,1,0:T(8,128)S(1)} %get-tuple-element.13.meta_ref), custom_call_target="tpu_custom_call" | custom-call | tf_op jit(solution)/shard_map/pallas_call | solution.py:399
  53.2 0.0 copy-done.2
  53.2 28.5 %shard_map.104 = (bf16[256,512]{1,0:T(8,128)(2,1)S(1)}, bf16[256,512]{1,0:T(8,128)(2,1)S(1)}, bf16[256,512]{1,0:T(8,128)(2,1)S(1)}, bf16[256,512]{1,0:T(8,128)(2,1)S(1)}) custom-call(bf16[8,4,128,128]{3,2,1,0:T(8,128)(2,1)S(1)} %get-tuple-element.14.y_ref, f32[8,2,8,128]{3,2,1,0:T(8,128)S(1)} %get-tuple-element.15.pw_ref, bf16[256,512]{1,0:T(8,128)(2,1)S(1)} %copy-done, ...), custom_call_target="tpu_custom_call" | custom-call | tf_op jit(solution)/shard_map/pallas_call | solution.py:410
  81.7 0.7 copy.16
  82.4 0.7 copy.17
  83.1 0.7 copy.18
  83.8 0.7 copy.19
  (2 shorter events, 0.0 us)
Async XLA Ops:
  0.6 0.7 copy-start.7
  1.3 0.7 copy-start.6
  2.0 0.7 copy-start.5
  2.7 0.9 %copy-start = (bf16[256,512]{1,0:T(8,128)(2,1)S(1)}, bf16[256,512]{1,0:T(8,128)(2,1)}, u32[]{:S(2)}) copy-start(bf16[256,512]{1,0:T(8,128)(2,1)} %q_ref.3) | copy-start | bytes 786436
  3.7 0.9 %copy-start.1 = (bf16[256,512]{1,0:T(8,128)(2,1)S(1)}, bf16[256,512]{1,0:T(8,128)(2,1)}, u32[]{:S(2)}) copy-start(bf16[256,512]{1,0:T(8,128)(2,1)} %g_ref.3) | copy-start | bytes 786436
  4.6 0.9 %copy-start.3 = (bf16[256,512]{1,0:T(8,128)(2,1)S(1)}, bf16[256,512]{1,0:T(8,128)(2,1)}, u32[]{:S(2)}) copy-start(bf16[256,512]{1,0:T(8,128)(2,1)} %k_ref.1) | copy-start | bytes 786436
  5.6 0.9 %copy-start.4 = (bf16[256,512]{1,0:T(8,128)(2,1)S(1)}, bf16[256,512]{1,0:T(8,128)(2,1)}, u32[]{:S(2)}) copy-start(bf16[256,512]{1,0:T(8,128)(2,1)} %v_ref.1) | copy-start | bytes 786436
  38.9 14.3 %copy-start.2 = (bf16[256,512]{1,0:T(8,128)(2,1)S(1)}, bf16[256,512]{1,0:T(8,128)(2,1)}, u32[]{:S(2)}) copy-start(bf16[256,512]{1,0:T(8,128)(2,1)} %g_ref.3) | copy-start | bytes 786436

commit v2 on v1

v2 whole, which is shorter than its diff:
```python
import functools

import jax
import jax.numpy as jnp
from jax import lax
from jax.experimental import pallas as pl
from jax.experimental.pallas import tpu as pltpu
from jax.sharding import PartitionSpec as P

HEADS = 8
HEAD_DIM = 64
BLOCK = 128
TMAX = 6
ROUNDS = 2
NEG_BIG = -1e30
SCALE = HEAD_DIM**-0.5
MESH = pl.DeviceIdType.MESH
VMEM = pltpu.VMEM
F32 = jnp.float32
BF16 = jnp.bfloat16
LIMIT = 56 * 1024 * 1024


def grp_offsets(clusters):
    found = set()
    for step in range(ROUNDS):
        found.add((step + 1) % clusters)
        found.add((-step - 1) % clusters)
    return sorted(found - {0})


def greet(clusters, team, row, me):
    barrier = pltpu.get_barrier_semaphore()
    offsets = grp_offsets(clusters)
    for offset in offsets:
        pl.semaphore_signal(
            barrier,
            inc=1,
            device_id=(lax.rem(row + offset, clusters), me),
            device_id_type=MESH,
        )
    for offset in range(1, team):
        pl.semaphore_signal(
            barrier, inc=1, device_id=(row, lax.rem(me + offset, team)), device_id_type=MESH
        )
    return barrier, len(offsets) + team - 1


def remote(src, dst, send_sem, recv_sem, target):
    return pltpu.make_async_remote_copy(
        src_ref=src,
        dst_ref=dst,
        send_sem=send_sem,
        recv_sem=recv_sem,
        device_id=target,
        device_id_type=MESH,
    )


def head_marks(rows, slot, width):
    at = lax.broadcasted_iota(jnp.int32, (rows, width), 0)
    column = lax.broadcasted_iota(jnp.int32, (rows, width), 1)
    hit = at == (column // HEAD_DIM) * 8 + slot
    return jnp.where(hit, 1.0, 0.0).astype(BF16)


def pick_rows(slots):
    at = lax.broadcasted_iota(jnp.int32, (BLOCK, BLOCK), 0)
    hit = jnp.where(at == jnp.broadcast_to(slots, (BLOCK, BLOCK)), 1.0, 0.0)
    return hit.T.astype(BF16)


def dot_last(left, right):
    return lax.dot_general(left, right, (((1,), (1,)), ((), ())), preferred_element_type=F32)


def dot(left, right):
    return jnp.dot(left, right, preferred_element_type=F32)


def fused_kernel(
    clusters,
    team,
    q_hbm,
    k_hbm,
    v_hbm,
    g_hbm,
    partner_ref,
    meta_ref,
    out_ref,
    dq_ref,
    dk_ref,
    dv_ref,
    near,
    far,
    qg_out,
    kv_out,
    qg_in,
    kv_in,
    pair_out,
    pair_in,
    meta_in,
    meta_s,
    picked,
    qg2,
    kvt,
    zw_all,
    oq_out,
    oq_in,
    dkv_out,
    dkv_in,
    pw_out,
    pw_in,
    pw_far,
    load_sem,
    meta_sem,
    qg_send,
    qg_recv,
    kv_send,
    kv_recv,
    m_send,
    m_recv,
    p_send,
    p_recv,
    o_send,
    o_recv,
    d_send,
    d_recv,
    w_send,
    w_recv,
    g_send,
    g_recv,
    f_send,
    f_recv,
):
    row = lax.axis_index("grp")
    me = lax.axis_index("blk")
    width = q_hbm.shape[1]
    blocks = 2 * team
    barrier, count = greet(clusters, team, row, me)
    q_at, k_at, v_at, g_at = range(4)

    loads = [
        pltpu.make_async_copy(src, near.at[at], load_sem.at[at])
        for at, src in enumerate((q_hbm, k_hbm, v_hbm, g_hbm))
    ]
    for load in loads:
        load.start()
    for load in loads:
        load.wait()

    def after(offset):
        return lax.rem(me + offset, team)

    def before(offset):
        return lax.rem(me + team - offset, team)

    def pack(out, one, two):
        for head in range(team):
            cols = slice(head * HEAD_DIM, (head + 1) * HEAD_DIM)
            for half in range(2):
                rows = slice(half * BLOCK, (half + 1) * BLOCK)
                out[head, half] = jnp.concatenate([near[one, rows, cols], near[two, rows, cols]], 1)

    pack(kv_out, k_at, v_at)
    pl.semaphore_wait(barrier, count)

    def across(out, into, send, recv, offset):
        peer = after(offset)
        return remote(out.at[peer], into.at[me], send.at[offset], recv.at[offset], (row, peer))

    def back_to(out, into, send, recv, offset):
        peer = before(offset)
        return remote(out.at[peer], into.at[me], send.at[offset], recv.at[offset], (row, peer))

    def matched(at, step, half):
        by = step + 1
        shift = by if half == 1 else clusters - by
        index = (at * ROUNDS + step) * 2 + half
        rows = pl.ds((1 - half) * BLOCK, BLOCK)
        return remote(
            near.at[at, rows],
            far.at[at, step, half],
            g_send.at[index],
            g_recv.at[index],
            (lax.rem(row + shift, clusters), me),
        )

    def meta_move(offset):
        peer = after(offset)
        return remote(
            meta_ref, meta_in.at[me], m_send.at[offset], m_recv.at[offset], (row, peer)
        )

    def all_matched(kinds):
        return [matched(at, step, half) for at in kinds for step in range(ROUNDS) for half in range(2)]

    metas = [meta_move(offset) for offset in range(1, team)]
    kv_moves = [across(kv_out, kv_in, kv_send, kv_recv, offset) for offset in range(1, team)]
    qg_moves = [across(qg_out, qg_in, qg_send, qg_recv, offset) for offset in range(1, team)]
    first = all_matched((k_at, v_at))
    second = all_matched((q_at, g_at))
    for copy in metas + first + kv_moves:
        copy.start()
    pack(qg_out, q_at, g_at)
    for copy in qg_moves + second:
        copy.start()
    kv_in[me] = kv_out[me]
    qg_in[me] = qg_out[me]
    meta_in[me] = meta_ref[...]
    zw_all[blocks * TMAX] = jnp.zeros((BLOCK, 2 * BLOCK), BF16)
    for copy in metas:
        copy.wait()
    to_scalar = pltpu.make_async_copy(meta_in, meta_s, meta_sem)
    to_scalar.start()
    to_scalar.wait()
    for copy in kv_moves:
        copy.wait()

    def turn(unit, carry):
        for half in range(2):
            kvt[2 * unit + half] = kv_in[unit, half].astype(F32).T.astype(BF16)
        return carry

    lax.fori_loop(0, team, turn, 0)

    for copy in first:
        copy.wait()
    marks = [head_marks(8 * HEADS, slot, width) for slot in range(2 * ROUNDS)]
    for half in range(2):
        rows = slice(half * BLOCK, (half + 1) * BLOCK)
        total = None
        for step in range(ROUNDS):
            pick = pick_rows(partner_ref[step : step + 1, rows])
            for at, (kind, own) in enumerate(((k_at, q_at), (v_at, g_at))):
                taken = dot(pick, far[kind, step, half])
                picked[at, step, rows] = taken.astype(BF16)
                product = near[own, rows].astype(F32) * taken
                high = product.astype(BF16)
                low = (product - high.astype(F32)).astype(BF16)
                mark = marks[at * ROUNDS + step]
                part = dot_last(mark, high) + dot_last(mark, low)
                total = part if total is None else total + part
        pair_out[:, half] = total.reshape(HEADS, 8, BLOCK)
    pairs = [across(pair_out, pair_in, p_send, p_recv, offset) for offset in range(1, team)]
    for copy in pairs:
        copy.start()
    pair_in[me] = pair_out[me]

    lane = lax.broadcasted_iota(jnp.int32, (BLOCK, BLOCK), 1) < HEAD_DIM

    def attend(unit, half):
        block = 2 * unit + half
        qg = qg_in[unit, half].astype(F32)
        split = jnp.concatenate([jnp.where(lane, qg, 0.0), jnp.where(lane, 0.0, qg)], 0)
        split = split.astype(BF16)
        qg2[block] = split
        ids = [meta_s[unit, half, slot] for slot in range(TMAX)]
        live = meta_s[unit, half, TMAX]
        pair = pair_in[unit, half]
        s_pair = [pair[r : r + 1] * SCALE for r in range(ROUNDS)]
        d_pair = [pair[ROUNDS + r : ROUNDS + r + 1] for r in range(ROUNDS)]
        s_loc, d_loc = [], []
        top = functools.reduce(jnp.maximum, s_pair)
        for slot in range(TMAX):
            kv = kv_in[ids[slot] // 2, ids[slot] % 2]
            both = dot_last(kv, split)
            scores = both[:, :BLOCK] * SCALE + jnp.where(slot < live, 0.0, NEG_BIG)
            s_loc.append(scores)
            d_loc.append(both[:, BLOCK:])
            top = jnp.maximum(top, jnp.max(scores, 0, keepdims=True))
        e_pair = [jnp.exp(s - top) for s in s_pair]
        total = functools.reduce(jnp.add, e_pair)
        e_loc = []
        for slot in range(TMAX):
            e = jnp.exp(s_loc[slot] - top)
            e_loc.append(e)
            total = total + jnp.sum(e, 0, keepdims=True)
        inverse = 1.0 / total
        p_pair = [e * inverse for e in e_pair]
        w_pair = [p.astype(BF16).astype(F32) for p in p_pair]
        delta = functools.reduce(jnp.add, [w * d for w, d in zip(w_pair, d_pair)])
        p_loc, w_loc = [], []
        for slot in range(TMAX):
            p = e_loc[slot] * inverse
            w = p.astype(BF16)
            p_loc.append(p)
            w_loc.append(w)
            delta = delta + jnp.sum(w.astype(F32) * d_loc[slot], 0, keepdims=True)
        z_pair = [(p * (d - delta)).astype(BF16).astype(F32) for p, d in zip(p_pair, d_pair)]
        pw_out[unit, half] = jnp.concatenate(
            w_pair + z_pair + [jnp.zeros((8 - 2 * ROUNDS, BLOCK), F32)], 0
        )
        back = None
        for slot in range(TMAX):
            z = (p_loc[slot] * (d_loc[slot] - delta)).astype(BF16)
            zw = jnp.concatenate([z, w_loc[slot]], 1)
            zw_all[block * TMAX + slot] = zw
            part = dot(kvt[ids[slot]], zw)
            back = part if back is None else back + part
        turned = jnp.concatenate([back[:HEAD_DIM, :BLOCK] * SCALE, back[HEAD_DIM:, BLOCK:]], 0)
        oq_out[unit, half] = turned.T.astype(BF16)

    def attend_unit(offset, carry):
        unit = before(offset)

        @pl.when(offset > 0)
        def _():
            across(qg_out, qg_in, qg_send, qg_recv, offset).wait()
            across(pair_out, pair_in, p_send, p_recv, offset).wait()

        for half in range(2):
            attend(unit, half)

        @pl.when(offset > 0)
        def _():
            back_to(pw_out, pw_in, w_send, w_recv, offset).start()
            back_to(oq_out, oq_in, o_send, o_recv, offset).start()

        return carry

    lax.fori_loop(0, team, attend_unit, 0)
    pw_in[me] = pw_out[me]
    oq_in[me] = oq_out[me]

    def key_grads(at, carry):
        offset = lax.rem(at + 1, team)
        unit = before(offset)
        for half in range(2):
            block = 2 * unit + half
            live = meta_s[unit, half, TMAX]
            total = None
            for slot in range(TMAX):
                other = meta_s[unit, half, slot]
                place = jnp.int32(0)
                for there in range(1, TMAX):
                    same = meta_s[other // 2, other % 2, there] == block
                    place = jnp.where(same, jnp.int32(there), place)
                index = jnp.where(slot < live, other * TMAX + place, blocks * TMAX)
                part = dot(zw_all[index], qg2[other])
                total = part if total is None else total + part
            dkv_out[unit, half] = jnp.where(lane, total * SCALE, total).astype(BF16)

        @pl.when(offset > 0)
        def _():
            back_to(dkv_out, dkv_in, d_send, d_recv, offset).start()

        return carry

    lax.fori_loop(0, team, key_grads, 0)
    dkv_in[me] = dkv_out[me]

    for offset in range(1, team):
        back_to(pw_out, pw_in, w_send, w_recv, offset).wait()
    forwards = []
    for step in range(ROUNDS):
        by = step + 1
        for half in range(2):
            shift = by if half == 0 else clusters - by
            index = step * 2 + half
            copy = remote(
                pw_in.at[:, half],
                pw_far.at[step, 1 - half],
                f_send.at[index],
                f_recv.at[index],
                (lax.rem(row + shift, clusters), me),
            )
            copy.start()
            forwards.append(copy)
    marks = [head_marks(BLOCK, slot, width) for slot in range(2 * ROUNDS)]

    def by_node(flat):
        flat = flat.reshape(8 * HEADS, BLOCK)
        flat = jnp.concatenate([flat, jnp.zeros((BLOCK - 8 * HEADS, BLOCK), F32)], 0)
        return flat.T.astype(BF16)

    def heads_of(buf, half, left):
        parts = [buf[head, half][:, left : left + HEAD_DIM] for head in range(team)]
        return jnp.concatenate(parts, 1).astype(F32)

    for offset in range(1, team):
        back_to(oq_out, oq_in, o_send, o_recv, offset).wait()
    for half in range(2):
        rows = slice(half * BLOCK, (half + 1) * BLOCK)
        turned = by_node(pw_in[:, half])
        attended = heads_of(oq_in, half, HEAD_DIM)
        query_grad = heads_of(oq_in, half, 0)
        for step in range(ROUNDS):
            w = dot(turned, marks[step])
            z = dot(turned, marks[ROUNDS + step]) * SCALE
            attended += w * picked[1, step, rows].astype(F32)
            query_grad += z * picked[0, step, rows].astype(F32)
        out_ref[rows] = attended.astype(BF16)
        dq_ref[rows] = query_grad.astype(BF16)

    for copy in second + forwards:
        copy.wait()
    backs = []
    for half in range(2):
        rows = slice(half * BLOCK, (half + 1) * BLOCK)
        back_key, back_value = None, None
        for step in range(ROUNDS):
            turned = by_node(pw_far[step, half])
            pick = pick_rows(partner_ref[step : step + 1, rows])
            w = dot(turned, marks[step])
            z = dot(turned, marks[ROUNDS + step]) * SCALE
            term_key = (z * far[q_at, step, half].astype(F32)).astype(BF16)
            term_value = (w * far[g_at, step, half].astype(F32)).astype(BF16)
            part_key, part_value = dot(pick, term_key), dot(pick, term_value)
            back_key = part_key if back_key is None else back_key + part_key
            back_value = part_value if back_value is None else back_value + part_value
        backs.append((back_key, back_value))
    for offset in range(1, team):
        back_to(dkv_out, dkv_in, d_send, d_recv, offset).wait()
    for half in range(2):
        rows = slice(half * BLOCK, (half + 1) * BLOCK)
        dk_ref[rows] = (heads_of(dkv_in, half, 0) + backs[half][0]).astype(BF16)
        dv_ref[rows] = (heads_of(dkv_in, half, HEAD_DIM) + backs[half][1]).astype(BF16)


def shards(clusters, team, query, key, value, out_grad, partner, tiles, tile_count):
    nodes, width = query.shape
    meta = jnp.concatenate([tiles, tile_count[:, None]], 1)
    meta = jnp.pad(meta, ((0, 8 - meta.shape[0]), (0, 128 - meta.shape[1])))
    shape = jax.ShapeDtypeStruct
    whole = pl.BlockSpec(memory_space=VMEM)
    dma = pltpu.SemaphoreType.DMA
    blocks = 2 * team
    big = VMEM((team, 2, BLOCK, BLOCK), BF16)
    few = VMEM((team, 2, 8, BLOCK), F32)
    metas = (team, 8, 128)
    return pl.pallas_call(
        functools.partial(fused_kernel, clusters, team),
        out_shape=(shape((nodes, width), BF16),) * 4,
        in_specs=[pl.BlockSpec(memory_space=pl.ANY)] * 4 + [whole] * 2,
        out_specs=(whole,) * 4,
        scratch_shapes=[
            VMEM((4, nodes, width), BF16),
            VMEM((4, ROUNDS, 2, BLOCK, width), BF16),
            big,
            big,
            big,
            big,
            few,
            few,
            VMEM(metas, jnp.int32),
            pltpu.SMEM(metas, jnp.int32),
            VMEM((2, ROUNDS, nodes, width), BF16),
            VMEM((blocks, 2 * BLOCK, BLOCK), BF16),
            VMEM((blocks, BLOCK, BLOCK), BF16),
            VMEM((blocks * TMAX + 1, BLOCK, 2 * BLOCK), BF16),
            big,
            big,
            big,
            big,
            few,
            few,
            VMEM((ROUNDS, 2, team, 8, BLOCK), F32),
            dma((4,)),
            dma,
        ]
        + [dma((team,))] * 14
        + [dma((8 * ROUNDS,))] * 2
        + [dma((2 * ROUNDS,))] * 2,
        compiler_params=pltpu.CompilerParams(
            collective_id=0, has_side_effects=True, vmem_limit_bytes=LIMIT
        ),
    )(query, key, value, out_grad, partner, meta)


def solution(mesh):
    rows = P(("grp", "blk"), None)
    in_specs = (rows, rows, rows, rows, P(None, ("grp", "blk")), rows, P(("grp", "blk")))
    return jax.shard_map(
        functools.partial(shards, mesh.shape["grp"], mesh.shape["blk"]),
        mesh=mesh,
        in_specs=in_specs,
        out_specs=(rows,) * 4,
        check_vma=False,
    )
```

time: 84.8 us -> 68.4 us (0.81)
  Pallas kernels: 75.2 us -> 61 us
  local copies, waits for them, and re-layouts: 8.62 us -> 6.43 us
    pallas_call x3 -> x1, Pallas kernels: 75.2 us -> 61 us  [shards(): pl.pallas_call(functools.partial(fused_kernel, clusters, team), out_shape...]
    unnamed x20 -> x14, local copies, waits for them, and re-layouts: 8.52 us -> 5.74 us
where the time goes in v2:
time: 68.4 us; the launch traced here: 68.1 us
  Pallas kernels  61 us (89%)
  local copies, waits for them, and re-layouts  6.43 us (9%)
    pallas_call x1, Pallas kernels, shards(): pl.pallas_call(functools.partial(fused_kernel, clusters, team), out_shape...  61 us
    unnamed x14, local copies, waits for them, and re-layouts  5.74 us

profile of v2, /device:TPU:0, one launch (start us, length us, event | category | flops | bytes accessed | tf_op | source)
XLA Modules:
  0.0 68.1 jit_solution(6864461753287227475)
XLA Ops:
  0.6 0.0 copy-start.4
  0.6 0.6 copy-done.4
  1.3 0.0 copy-start.3
  1.3 0.1 copy.11
  1.4 0.6 copy-done.3
  2.0 0.1 pad_add_fusion
  2.0 0.6 pad.4.meta_ref
  2.6 61.0 %shard_map.102 = (bf16[256,512]{1,0:T(8,128)(2,1)}, bf16[256,512]{1,0:T(8,128)(2,1)}, bf16[256,512]{1,0:T(8,128)(2,1)}, bf16[256,512]{1,0:T(8,128)(2,1)}) custom-call(bf16[256,512]{1,0:T(8,128)(2,1)} %q_hbm.1, bf16[256,512]{1,0:T(8,128)(2,1)} %k_hbm.1, bf16[256,512]{1,0:T(8,128)(2,1)} %v_hbm.1, bf16[256,512]{1,0:T(8,128)(2,1)} %g_hbm.1, ...), custom_call_target="tpu_custom_call" | custom-call | tf_op jit(solution)/shard_map/pallas_call | solution.py:432
  63.6 0.0 copy-start.2
  63.6 1.7 %copy.16 = bf16[256,512]{1,0:T(8,128)(2,1)} copy(bf16[256,512]{1,0:T(8,128)(2,1)} %get-tuple-element.8) | data formatting | bytes 524288
  65.4 0.0 copy-done.2
  65.4 0.0 copy-start.1
  65.4 0.7 %copy.17 = bf16[256,512]{1,0:T(8,128)(2,1)} copy(bf16[256,512]{1,0:T(8,128)(2,1)S(1)} %copy-done.2) | data formatting | bytes 524288
  66.1 0.3 copy-done.1
  66.4 0.0 copy-start
  66.4 0.7 %copy.18 = bf16[256,512]{1,0:T(8,128)(2,1)} copy(bf16[256,512]{1,0:T(8,128)(2,1)S(1)} %copy-done.1) | data formatting | bytes 524288
  67.1 0.3 copy-done
  67.4 0.7 %copy.19 = bf16[256,512]{1,0:T(8,128)(2,1)} copy(bf16[256,512]{1,0:T(8,128)(2,1)S(1)} %copy-done) | data formatting | bytes 524288
Async XLA Ops:
  0.6 0.7 copy-start.4
  1.3 0.7 copy-start.3
  63.6 1.7 %copy-start.2 = (bf16[256,512]{1,0:T(8,128)(2,1)S(1)}, bf16[256,512]{1,0:T(8,128)(2,1)}, u32[]{:S(2)}) copy-start(bf16[256,512]{1,0:T(8,128)(2,1)} %get-tuple-element.9) | copy-start | bytes 786436
  65.4 1.0 %copy-start.1 = (bf16[256,512]{1,0:T(8,128)(2,1)S(1)}, bf16[256,512]{1,0:T(8,128)(2,1)}, u32[]{:S(2)}) copy-start(bf16[256,512]{1,0:T(8,128)(2,1)} %get-tuple-element.10) | copy-start | bytes 786436
  66.4 1.0 %copy-start = (bf16[256,512]{1,0:T(8,128)(2,1)S(1)}, bf16[256,512]{1,0:T(8,128)(2,1)}, u32[]{:S(2)}) copy-start(bf16[256,512]{1,0:T(8,128)(2,1)} %get-tuple-element.11) | copy-start | bytes 786436

commit v3 on v2

--- a/solution.py
+++ b/solution.py
@@ -85,14 +85,17 @@
     k_hbm,
     v_hbm,
     g_hbm,
-    partner_ref,
-    meta_ref,
+    partner_hbm,
+    tiles_ref,
+    count_ref,
     out_ref,
     dq_ref,
     dk_ref,
     dv_ref,
     near,
     far,
+    partner_ref,
+    meta_ref,
     qg_out,
     kv_out,
     qg_in,
@@ -105,6 +108,9 @@
     qg2,
     kvt,
     zw_all,
+    e_all,
+    d_all,
+    stats,
     oq_out,
     oq_in,
     dkv_out,
@@ -144,8 +150,17 @@
         pltpu.make_async_copy(src, near.at[at], load_sem.at[at])
         for at, src in enumerate((q_hbm, k_hbm, v_hbm, g_hbm))
     ]
+    loads.append(pltpu.make_async_copy(partner_hbm, partner_ref, load_sem.at[4]))
     for load in loads:
         load.start()
+    down = lax.broadcasted_iota(jnp.int32, (8, 128), 0)
+    right = lax.broadcasted_iota(jnp.int32, (8, 128), 1)
+    meta = jnp.zeros((8, 128), jnp.int32)
+    for half in range(2):
+        for slot in range(TMAX):
+            meta = jnp.where((down == half) & (right == slot), tiles_ref[half, slot], meta)
+        meta = jnp.where((down == half) & (right == TMAX), count_ref[half], meta)
+    meta_ref[...] = meta
     for load in loads:
         load.wait()
 
@@ -223,6 +238,50 @@
         return carry
 
     lax.fori_loop(0, team, turn, 0)
+
+    lane = lax.broadcasted_iota(jnp.int32, (BLOCK, BLOCK), 1) < HEAD_DIM
+
+    def attend_local(unit, half):
+        block = 2 * unit + half
+        qg = qg_in[unit, half].astype(F32)
+        split = jnp.concatenate([jnp.where(lane, qg * SCALE, 0.0), jnp.where(lane, 0.0, qg)], 0)
+        split = split.astype(BF16)
+        qg2[block] = split
+        live = meta_s[unit, half, TMAX]
+        s_loc = []
+        top = None
+        for slot in range(TMAX):
+            source = meta_s[unit, half, slot]
+            both = dot_last(kv_in[source // 2, source % 2], split)
+            scores = both[:, :BLOCK] + jnp.where(slot < live, 0.0, NEG_BIG)
+            s_loc.append(scores)
+            d_all[block * TMAX + slot] = both[:, BLOCK:]
+            most = jnp.max(scores, 0, keepdims=True)
+            top = most if top is None else jnp.maximum(top, most)
+        total, weighted = None, None
+        for slot in range(TMAX):
+            e = jnp.exp(s_loc[slot] - top)
+            e_all[block * TMAX + slot] = e
+            part = jnp.sum(e, 0, keepdims=True)
+            other = jnp.sum(e * d_all[block * TMAX + slot], 0, keepdims=True)
+            total = part if total is None else total + part
+            weighted = other if weighted is None else weighted + other
+        stats[block] = jnp.concatenate(
+            [top, total, weighted, jnp.zeros((5, BLOCK), F32)], 0
+        )
+
+    def local_unit(offset, carry):
+        unit = before(offset)
+
+        @pl.when(offset > 0)
+        def _():
+            across(qg_out, qg_in, qg_send, qg_recv, offset).wait()
+
+        for half in range(2):
+            attend_local(unit, half)
+        return carry
+
+    lax.fori_loop(0, team // 2, local_unit, 0)
 
     for copy in first:
         copy.wait()
@@ -247,54 +306,35 @@
         copy.start()
     pair_in[me] = pair_out[me]
 
-    lane = lax.broadcasted_iota(jnp.int32, (BLOCK, BLOCK), 1) < HEAD_DIM
-
-    def attend(unit, half):
+    lax.fori_loop(team // 2, team, local_unit, 0)
+
+    def attend_pair(unit, half):
         block = 2 * unit + half
-        qg = qg_in[unit, half].astype(F32)
-        split = jnp.concatenate([jnp.where(lane, qg, 0.0), jnp.where(lane, 0.0, qg)], 0)
-        split = split.astype(BF16)
-        qg2[block] = split
         ids = [meta_s[unit, half, slot] for slot in range(TMAX)]
-        live = meta_s[unit, half, TMAX]
+        held = stats[block]
+        top_loc, total_loc, dot_loc = held[0:1], held[1:2], held[2:3]
         pair = pair_in[unit, half]
         s_pair = [pair[r : r + 1] * SCALE for r in range(ROUNDS)]
         d_pair = [pair[ROUNDS + r : ROUNDS + r + 1] for r in range(ROUNDS)]
-        s_loc, d_loc = [], []
-        top = functools.reduce(jnp.maximum, s_pair)
-        for slot in range(TMAX):
-            kv = kv_in[ids[slot] // 2, ids[slot] % 2]
-            both = dot_last(kv, split)
-            scores = both[:, :BLOCK] * SCALE + jnp.where(slot < live, 0.0, NEG_BIG)
-            s_loc.append(scores)
-            d_loc.append(both[:, BLOCK:])
-            top = jnp.maximum(top, jnp.max(scores, 0, keepdims=True))
+        top = functools.reduce(jnp.maximum, s_pair, top_loc)
+        shrink = jnp.exp(top_loc - top)
         e_pair = [jnp.exp(s - top) for s in s_pair]
-        total = functools.reduce(jnp.add, e_pair)
-        e_loc = []
-        for slot in range(TMAX):
-            e = jnp.exp(s_loc[slot] - top)
-            e_loc.append(e)
-            total = total + jnp.sum(e, 0, keepdims=True)
-        inverse = 1.0 / total
+        inverse = 1.0 / functools.reduce(jnp.add, e_pair, total_loc * shrink)
+        factor = shrink * inverse
         p_pair = [e * inverse for e in e_pair]
+        delta = functools.reduce(
+            jnp.add, [p * d for p, d in zip(p_pair, d_pair)], dot_loc * factor
+        )
         w_pair = [p.astype(BF16).astype(F32) for p in p_pair]
-        delta = functools.reduce(jnp.add, [w * d for w, d in zip(w_pair, d_pair)])
-        p_loc, w_loc = [], []
-        for slot in range(TMAX):
-            p = e_loc[slot] * inverse
-            w = p.astype(BF16)
-            p_loc.append(p)
-            w_loc.append(w)
-            delta = delta + jnp.sum(w.astype(F32) * d_loc[slot], 0, keepdims=True)
         z_pair = [(p * (d - delta)).astype(BF16).astype(F32) for p, d in zip(p_pair, d_pair)]
         pw_out[unit, half] = jnp.concatenate(
             w_pair + z_pair + [jnp.zeros((8 - 2 * ROUNDS, BLOCK), F32)], 0
         )
         back = None
         for slot in range(TMAX):
-            z = (p_loc[slot] * (d_loc[slot] - delta)).astype(BF16)
-            zw = jnp.concatenate([z, w_loc[slot]], 1)
+            p = e_all[block * TMAX + slot] * factor
+            z = (p * (d_all[block * TMAX + slot] - delta)).astype(BF16)
+            zw = jnp.concatenate([z, p.astype(BF16)], 1)
             zw_all[block * TMAX + slot] = zw
             part = dot(kvt[ids[slot]], zw)
             back = part if back is None else back + part
@@ -306,11 +346,10 @@
 
         @pl.when(offset > 0)
         def _():
-            across(qg_out, qg_in, qg_send, qg_recv, offset).wait()
             across(pair_out, pair_in, p_send, p_recv, offset).wait()
 
         for half in range(2):
-            attend(unit, half)
+            attend_pair(unit, half)
 
         @pl.when(offset > 0)
         def _():
@@ -339,7 +378,7 @@
                 index = jnp.where(slot < live, other * TMAX + place, blocks * TMAX)
                 part = dot(zw_all[index], qg2[other])
                 total = part if total is None else total + part
-            dkv_out[unit, half] = jnp.where(lane, total * SCALE, total).astype(BF16)
+            dkv_out[unit, half] = total.astype(BF16)
 
         @pl.when(offset > 0)
         def _():
@@ -418,25 +457,36 @@
         dv_ref[rows] = (heads_of(dkv_in, half, HEAD_DIM) + backs[half][1]).astype(BF16)
 
 
+def write_kernel(*refs):
+    sems = refs[8]
+    copies = [pltpu.make_async_copy(refs[at], refs[4 + at], sems.at[at]) for at in range(4)]
+    for copy in copies:
+        copy.start()
+    for copy in copies:
+        copy.wait()
+
+
 def shards(clusters, team, query, key, value, out_grad, partner, tiles, tile_count):
     nodes, width = query.shape
-    meta = jnp.concatenate([tiles, tile_count[:, None]], 1)
-    meta = jnp.pad(meta, ((0, 8 - meta.shape[0]), (0, 128 - meta.shape[1])))
     shape = jax.ShapeDtypeStruct
     whole = pl.BlockSpec(memory_space=VMEM)
+    scalar = pl.BlockSpec(memory_space=pltpu.SMEM)
+    anywhere = pl.BlockSpec(memory_space=pl.ANY)
     dma = pltpu.SemaphoreType.DMA
     blocks = 2 * team
     big = VMEM((team, 2, BLOCK, BLOCK), BF16)
     few = VMEM((team, 2, 8, BLOCK), F32)
     metas = (team, 8, 128)
-    return pl.pallas_call(
+    results = pl.pallas_call(
         functools.partial(fused_kernel, clusters, team),
         out_shape=(shape((nodes, width), BF16),) * 4,
-        in_specs=[pl.BlockSpec(memory_space=pl.ANY)] * 4 + [whole] * 2,
+        in_specs=[anywhere] * 5 + [scalar] * 2,
         out_specs=(whole,) * 4,
         scratch_shapes=[
             VMEM((4, nodes, width), BF16),
             VMEM((4, ROUNDS, 2, BLOCK, width), BF16),
+            VMEM((ROUNDS, nodes), jnp.int32),
+            VMEM((8, 128), jnp.int32),
             big,
             big,
             big,
@@ -449,6 +499,9 @@
             VMEM((blocks, 2 * BLOCK, BLOCK), BF16),
             VMEM((blocks, BLOCK, BLOCK), BF16),
             VMEM((blocks * TMAX + 1, BLOCK, 2 * BLOCK), BF16),
+            VMEM((blocks * TMAX, BLOCK, BLOCK), F32),
+            VMEM((blocks * TMAX, BLOCK, BLOCK), F32),
+            VMEM((blocks, 8, BLOCK), F32),
             big,
             big,
             big,
@@ -456,7 +509,7 @@
             few,
             few,
             VMEM((ROUNDS, 2, team, 8, BLOCK), F32),
-            dma((4,)),
+            dma((5,)),
             dma,
         ]
         + [dma((team,))] * 14
@@ -465,7 +518,14 @@
         compiler_params=pltpu.CompilerParams(
             collective_id=0, has_side_effects=True, vmem_limit_bytes=LIMIT
         ),
-    )(query, key, value, out_grad, partner, meta)
+    )(query, key, value, out_grad, partner, tiles, tile_count)
+    return pl.pallas_call(
+        write_kernel,
+        out_shape=(shape((nodes, width), BF16),) * 4,
+        in_specs=[anywhere] * 4,
+        out_specs=(anywhere,) * 4,
+        scratch_shapes=[dma((4,))],
+    )(*results)
 
 
 def solution(mesh):

time: 68.4 us -> 97.2 us (1.42)
  Pallas kernels: 61 us -> 96.4 us
  local copies, waits for them, and re-layouts: 6.43 us -> 0 us
    pallas_call x0 -> x1, Pallas kernels: none -> 32.9 us  [shards(): pl.pallas_call(write_kernel, out_shape=(shape((nodes, width), BF16),) * 4...]
    unnamed x14 -> x0, local copies, waits for them, and re-layouts: 5.74 us -> none
    pallas_call x1, Pallas kernels: 61 us -> 63.5 us  [shards(): pl.pallas_call(functools.partial(fused_kernel, clusters, team), out_shape...]
where the time goes in v3:
time: 97.2 us; the launch traced here: 97.1 us
  Pallas kernels  96.4 us (99%)
    pallas_call x1, Pallas kernels, shards(): pl.pallas_call(functools.partial(fused_kernel, clusters, team), out_shape...  63.5 us
    pallas_call x1, Pallas kernels, shards(): pl.pallas_call(write_kernel, out_shape=(shape((nodes, width), BF16),) * 4...  32.9 us

profile of v3, /device:TPU:0, one launch (start us, length us, event | category | flops | bytes accessed | tf_op | source)
XLA Modules:
  0.0 97.1 jit_solution(16468350089481177482)
XLA Ops:
  0.6 63.5 %shard_map.102 = (bf16[256,512]{1,0:T(8,128)(2,1)}, bf16[256,512]{1,0:T(8,128)(2,1)}, bf16[256,512]{1,0:T(8,128)(2,1)}, bf16[256,512]{1,0:T(8,128)(2,1)}) custom-call(bf16[256,512]{1,0:T(8,128)(2,1)} %q_hbm.1, bf16[256,512]{1,0:T(8,128)(2,1)} %k_hbm.1, bf16[256,512]{1,0:T(8,128)(2,1)} %v_hbm.1, bf16[256,512]{1,0:T(8,128)(2,1)} %g_hbm.1, ...), custom_call_target="tpu_custom_call" | custom-call | tf_op jit(solution)/shard_map/pallas_call | solution.py:480
  64.2 32.9 %shard_map.103 = (bf16[256,512]{1,0:T(8,128)(2,1)}, bf16[256,512]{1,0:T(8,128)(2,1)}, bf16[256,512]{1,0:T(8,128)(2,1)}, bf16[256,512]{1,0:T(8,128)(2,1)}) custom-call(bf16[256,512]{1,0:T(8,128)(2,1)} %get-tuple-element.8.refs_0_, bf16[256,512]{1,0:T(8,128)(2,1)} %get-tuple-element.9.refs_1_, bf16[256,512]{1,0:T(8,128)(2,1)} %get-tuple-element.10.refs_2_, ...), custom_call_target="tpu_custom_call" | custom-call | tf_op jit(solution)/shard_map/pallas_call | solution.py:522

commit v4 on v3

--- a/solution.py
+++ b/solution.py
@@ -218,7 +218,7 @@
     for copy in metas + first + kv_moves:
         copy.start()
     pack(qg_out, q_at, g_at)
-    for copy in qg_moves + second:
+    for copy in qg_moves:
         copy.start()
     kv_in[me] = kv_out[me]
     qg_in[me] = qg_out[me]
@@ -270,21 +270,13 @@
             [top, total, weighted, jnp.zeros((5, BLOCK), F32)], 0
         )
 
-    def local_unit(offset, carry):
-        unit = before(offset)
-
-        @pl.when(offset > 0)
-        def _():
-            across(qg_out, qg_in, qg_send, qg_recv, offset).wait()
-
-        for half in range(2):
-            attend_local(unit, half)
-        return carry
-
-    lax.fori_loop(0, team // 2, local_unit, 0)
+    for half in range(2):
+        attend_local(me, half)
 
     for copy in first:
         copy.wait()
+    for copy in second:
+        copy.start()
     marks = [head_marks(8 * HEADS, slot, width) for slot in range(2 * ROUNDS)]
     for half in range(2):
         rows = slice(half * BLOCK, (half + 1) * BLOCK)
@@ -306,8 +298,6 @@
         copy.start()
     pair_in[me] = pair_out[me]
 
-    lax.fori_loop(team // 2, team, local_unit, 0)
-
     def attend_pair(unit, half):
         block = 2 * unit + half
         ids = [meta_s[unit, half, slot] for slot in range(TMAX)]
@@ -346,6 +336,9 @@
 
         @pl.when(offset > 0)
         def _():
+            across(qg_out, qg_in, qg_send, qg_recv, offset).wait()
+            for half in range(2):
+                attend_local(unit, half)
             across(pair_out, pair_in, p_send, p_recv, offset).wait()
 
         for half in range(2):
@@ -458,12 +451,16 @@
 
 
 def write_kernel(*refs):
-    sems = refs[8]
-    copies = [pltpu.make_async_copy(refs[at], refs[4 + at], sems.at[at]) for at in range(4)]
+    held, in_sems, out_sems = refs[8:]
+    copies = [pltpu.make_async_copy(refs[at], held.at[at], in_sems.at[at]) for at in range(4)]
+    writes = [pltpu.make_async_copy(held.at[at], refs[4 + at], out_sems.at[at]) for at in range(4)]
     for copy in copies:
         copy.start()
-    for copy in copies:
+    for copy, write in zip(copies, writes):
         copy.wait()
+        write.start()
+    for write in writes:
+        write.wait()
 
 
 def shards(clusters, team, query, key, value, out_grad, partner, tiles, tile_count):
@@ -524,7 +521,7 @@
         out_shape=(shape((nodes, width), BF16),) * 4,
         in_specs=[anywhere] * 4,
         out_specs=(anywhere,) * 4,
-        scratch_shapes=[dma((4,))],
+        scratch_shapes=[VMEM((4, nodes, width), BF16), dma((4,)), dma((4,))],
     )(*results)
 
 

time: 97.2 us -> 63.4 us (0.65)
  Pallas kernels: 96.4 us -> 62.6 us
    pallas_call x1, Pallas kernels: 32.9 us -> 1.98 us  [shards(): pl.pallas_call(write_kernel, out_shape=(shape((nodes, width), BF16),) * 4...]
    pallas_call x1, Pallas kernels: 63.5 us -> 60.6 us  [shards(): pl.pallas_call(functools.partial(fused_kernel, clusters, team), out_shape...]
where the time goes in v4:
time: 63.4 us; the launch traced here: 63.2 us
  Pallas kernels  62.6 us (99%)
  between operations  0.64 us (1%)
    pallas_call x1, Pallas kernels, shards(): pl.pallas_call(functools.partial(fused_kernel, clusters, team), out_shape...  60.6 us
    pallas_call x1, Pallas kernels, shards(): pl.pallas_call(write_kernel, out_shape=(shape((nodes, width), BF16),) * 4...  1.98 us

profile of v4, /device:TPU:0, one launch (start us, length us, event | category | flops | bytes accessed | tf_op | source)
XLA Modules:
  0.0 63.2 jit_solution(16267867364916385553)
XLA Ops:
  0.6 60.6 %shard_map.102 = (bf16[256,512]{1,0:T(8,128)(2,1)}, bf16[256,512]{1,0:T(8,128)(2,1)}, bf16[256,512]{1,0:T(8,128)(2,1)}, bf16[256,512]{1,0:T(8,128)(2,1)}) custom-call(bf16[256,512]{1,0:T(8,128)(2,1)} %q_hbm.1, bf16[256,512]{1,0:T(8,128)(2,1)} %k_hbm.1, bf16[256,512]{1,0:T(8,128)(2,1)} %v_hbm.1, bf16[256,512]{1,0:T(8,128)(2,1)} %g_hbm.1, ...), custom_call_target="tpu_custom_call" | custom-call | tf_op jit(solution)/shard_map/pallas_call | solution.py:477
  61.3 2.0 %shard_map.103 = (bf16[256,512]{1,0:T(8,128)(2,1)}, bf16[256,512]{1,0:T(8,128)(2,1)}, bf16[256,512]{1,0:T(8,128)(2,1)}, bf16[256,512]{1,0:T(8,128)(2,1)}) custom-call(bf16[256,512]{1,0:T(8,128)(2,1)} %get-tuple-element.8.refs_0_, bf16[256,512]{1,0:T(8,128)(2,1)} %get-tuple-element.9.refs_1_, bf16[256,512]{1,0:T(8,128)(2,1)} %get-tuple-element.10.refs_2_, ...), custom_call_target="tpu_custom_call" | custom-call | tf_op jit(solution)/shard_map/pallas_call | solution.py:519

commit v5 on v4

--- a/solution.py
+++ b/solution.py
@@ -165,10 +165,13 @@
         load.wait()
 
     def after(offset):
-        return lax.rem(me + offset, team)
-
-    def before(offset):
-        return lax.rem(me + team - offset, team)
+        peer, bit = 0, 1
+        while bit < team:
+            peer = peer + bit * ((me // bit + offset // bit) % 2)
+            bit *= 2
+        return peer
+
+    before = after
 
     def pack(out, one, two):
         for head in range(team):
@@ -356,7 +359,7 @@
     oq_in[me] = oq_out[me]
 
     def key_grads(at, carry):
-        offset = lax.rem(at + 1, team)
+        offset = team - 1 - at
         unit = before(offset)
         for half in range(2):
             block = 2 * unit + half

time: 63.4 us -> 62.3 us (0.983)
  Pallas kernels: 62.6 us -> 61.5 us
    pallas_call x1, Pallas kernels: 60.6 us -> 59.5 us  [shards(): pl.pallas_call(functools.partial(fused_kernel, clusters, team), out_shape...]
where the time goes in v5:
time: 62.3 us; the launch traced here: 62.1 us
  Pallas kernels  61.5 us (99%)
  between operations  0.64 us (1%)
    pallas_call x1, Pallas kernels, shards(): pl.pallas_call(functools.partial(fused_kernel, clusters, team), out_shape...  59.5 us
    pallas_call x1, Pallas kernels, shards(): pl.pallas_call(write_kernel, out_shape=(shape((nodes, width), BF16),) * 4...  1.98 us

profile of v5, /device:TPU:0, one launch (start us, length us, event | category | flops | bytes accessed | tf_op | source)
XLA Modules:
  0.0 62.1 jit_solution(12517132515695166949)
XLA Ops:
  0.6 59.5 %shard_map.102 = (bf16[256,512]{1,0:T(8,128)(2,1)}, bf16[256,512]{1,0:T(8,128)(2,1)}, bf16[256,512]{1,0:T(8,128)(2,1)}, bf16[256,512]{1,0:T(8,128)(2,1)}) custom-call(bf16[256,512]{1,0:T(8,128)(2,1)} %q_hbm.1, bf16[256,512]{1,0:T(8,128)(2,1)} %k_hbm.1, bf16[256,512]{1,0:T(8,128)(2,1)} %v_hbm.1, bf16[256,512]{1,0:T(8,128)(2,1)} %g_hbm.1, ...), custom_call_target="tpu_custom_call" | custom-call | tf_op jit(solution)/shard_map/pallas_call | solution.py:480
  60.1 2.0 %shard_map.103 = (bf16[256,512]{1,0:T(8,128)(2,1)}, bf16[256,512]{1,0:T(8,128)(2,1)}, bf16[256,512]{1,0:T(8,128)(2,1)}, bf16[256,512]{1,0:T(8,128)(2,1)}) custom-call(bf16[256,512]{1,0:T(8,128)(2,1)} %get-tuple-element.8.refs_0_, bf16[256,512]{1,0:T(8,128)(2,1)} %get-tuple-element.9.refs_1_, bf16[256,512]{1,0:T(8,128)(2,1)} %get-tuple-element.10.refs_2_, ...), custom_call_target="tpu_custom_call" | custom-call | tf_op jit(solution)/shard_map/pallas_call | solution.py:522
